TPU v7x, 256 devices: a whole 4x4x8 slice. The times are simulated.
256 devices in a mesh: ctx: 32 (over y_lo, z, core), tp: 8 (over x, y_hi).
Axes of the slice: x: 4, y: 4 (y_hi: 2, y_lo: 2; y = y_hi * 2 + y_lo), z: 8, core: 2. Of those that a mesh axis runs over, the one named last changes fastest.
Arguments:
- queries: bfloat16 [8192, 4096], P('ctx', 'tp'), may hold values from -8 to 8
- key_cache: bfloat16 [131072, 1024], P('ctx', 'tp'), may hold values from -6 to 6
- values: bfloat16 [131072, 1024], P('ctx', 'tp'), may hold values from -6 to 6
- out_weight: bfloat16 [4096, 8192], P('tp'), may hold values from -0.09375 to 0.09375
- selected: int32 [512, 3], P('ctx'), may hold values from -1 to 30, as said below
- shard_order: int32 [32], replicated, may hold values from 0 to 31, each once
Outputs:
- trainer_view: bfloat16 [8192, 8192], P('ctx', 'tp')
Inputs may be any that keep to these rules, and one draw needn't show every extreme that they name: `selected`: the blocks a tile names are distinct and lie before the tile's own block; -1 stands for no block. Among the tiles of one block no earlier block is named more than 2 times, and in every draw some block names one exactly 2 times.
All inputs are finite; a program needn't handle non-finite values.
Results may differ from a plain program's by a relative error of at most 0.01555.
Values may be sent and summed in bfloat16 or wider, within the bound.
A program may use at most 128 MiB of HBM per device.

v0:
```python
import math

import jax
import jax.numpy as jnp
from jax import lax
from jax.sharding import PartitionSpec as P

H = 32
KVH = 8
DH = 128
BLOCK = 4096
TOPK = 3
TILE = 16
CAP = 2
QROWS = 256


def attend(query_rows, key_block, value_block, visible):
    kv_heads = query_rows.shape[0]
    head_size = query_rows.shape[2]
    key_rows = key_block.reshape(key_block.shape[0], kv_heads, head_size)
    value_rows = value_block.reshape(value_block.shape[0], kv_heads, head_size)
    scores = jnp.einsum(
        "jrd,kjd->jrk", query_rows, key_rows, preferred_element_type=jnp.float32
    ) * (1.0 / math.sqrt(head_size))
    if visible is not None:
        scores = jnp.where(visible, scores, -jnp.inf)
    row_peak = jnp.max(scores, axis=-1)
    weights = jnp.exp(scores - row_peak[..., None])
    row_mass = jnp.sum(weights, axis=-1)
    weighted = jnp.einsum(
        "jrk,kjd->jrd", weights.astype(jnp.bfloat16), value_rows, preferred_element_type=jnp.float32
    )
    return (weighted / row_mass[..., None], row_peak, row_mass)


def from_tiles(tiled):
    tile_count, tile_rows, kv_heads, groups, head_size = tiled.shape
    return tiled.transpose(2, 3, 0, 1, 4).reshape(
        kv_heads, groups * tile_count * tile_rows, head_size
    )


def to_tiles(field_rows, tile_count, tile_rows, kv_heads, groups):
    head_size = field_rows.shape[-1]
    shaped = field_rows.reshape(kv_heads, groups, tile_count, tile_rows, head_size).transpose(
        2, 3, 0, 1, 4
    )
    return shaped.reshape(tile_count, tile_rows, kv_heads * groups * head_size)


def stats_tiles(stat_rows, tile_count, tile_rows, kv_heads, groups):
    shaped = stat_rows.reshape(kv_heads, groups, tile_count, tile_rows).transpose(2, 0, 1, 3)
    return shaped.reshape(tile_count, kv_heads * groups, tile_rows)


def local(queries, key_cache, values, out_weight, selected, shard_order):
    ctx_size = lax.axis_size("ctx")
    kv_heads = key_cache.shape[1] // DH
    groups = H // KVH
    heads_dev = kv_heads * groups
    head_cols = queries.shape[1]
    tile_count = QROWS // TILE
    pair_count = tile_count * TOPK
    slot_total = ctx_size * CAP
    own_rows = from_tiles(queries.reshape(tile_count, TILE, kv_heads, groups, DH))
    position = BLOCK - QROWS + jnp.arange(groups * QROWS) % QROWS
    visible = jnp.arange(BLOCK)[None, None, :] <= position[None, :, None]
    own_mix, own_peak, own_mass = attend(own_rows, key_cache, values, visible)
    own_mix = to_tiles(own_mix, tile_count, TILE, kv_heads, groups).reshape(
        tile_count, TILE, heads_dev, DH
    )
    own_peak = stats_tiles(own_peak, tile_count, TILE, kv_heads, groups)
    own_mass = stats_tiles(own_mass, tile_count, TILE, kv_heads, groups)
    chosen = selected.reshape(pair_count)
    is_sent = chosen >= 0
    earlier = jnp.arange(pair_count)[None, :] < jnp.arange(pair_count)[:, None]
    same_dest = (chosen[:, None] == chosen[None, :]) & earlier & is_sent[None, :]
    slot_rank = jnp.sum(same_dest.astype(jnp.int32), axis=1)
    slot_index = jnp.where(is_sent, chosen * CAP + slot_rank, -1)
    dispatch = (jnp.arange(slot_total)[:, None] == slot_index[None, :]).reshape(
        slot_total, tile_count, TOPK
    )
    dispatch = jnp.sum(dispatch.astype(jnp.bfloat16), axis=2)
    outgoing = jnp.dot(
        dispatch, queries.reshape(tile_count, TILE * head_cols), preferred_element_type=jnp.float32
    )
    outgoing = outgoing.astype(jnp.bfloat16).reshape(ctx_size, CAP, TILE, head_cols)
    received = lax.all_to_all(outgoing, "ctx", split_axis=0, concat_axis=0, tiled=True)
    sources = received.shape[0]
    item_count = received.shape[1]
    slot_count = sources * item_count
    group_size = 8
    batches = received.reshape(slot_count // group_size, group_size, TILE, kv_heads, groups, DH)

    def serve_group(slot_batch):
        mixed_rows, row_peak, row_mass = attend(from_tiles(slot_batch), key_cache, values, None)
        return (
            to_tiles(mixed_rows, group_size, TILE, kv_heads, groups),
            stats_tiles(row_peak, group_size, TILE, kv_heads, groups),
            stats_tiles(row_mass, group_size, TILE, kv_heads, groups),
        )

    results = lax.map(serve_group, batches)
    back_mix = lax.all_to_all(
        results[0].reshape(sources, item_count, TILE, head_cols),
        "ctx",
        split_axis=0,
        concat_axis=0,
        tiled=True,
    )
    back_peak = lax.all_to_all(
        results[1].reshape(sources, item_count, heads_dev, TILE),
        "ctx",
        split_axis=0,
        concat_axis=0,
        tiled=True,
    )
    back_mass = lax.all_to_all(
        results[2].reshape(sources, item_count, heads_dev, TILE),
        "ctx",
        split_axis=0,
        concat_axis=0,
        tiled=True,
    )
    flat_index = jnp.clip(slot_index, 0, slot_total - 1)
    pair_mix = jnp.take(back_mix.reshape(slot_total, TILE, head_cols), flat_index, axis=0)
    pair_peak = jnp.take(back_peak.reshape(slot_total, heads_dev, TILE), flat_index, axis=0)
    pair_mass = jnp.take(back_mass.reshape(slot_total, heads_dev, TILE), flat_index, axis=0)
    in_use = is_sent.reshape(tile_count, TOPK)[:, :, None, None]
    pair_mix = pair_mix.reshape(tile_count, TOPK, TILE, heads_dev, DH)
    pair_peak = pair_peak.reshape(tile_count, TOPK, heads_dev, TILE)
    pair_mass = pair_mass.reshape(tile_count, TOPK, heads_dev, TILE)
    peak_all = jnp.maximum(
        own_peak, jnp.max(jnp.where(in_use, pair_peak, own_peak[:, None]), axis=1)
    )
    own_weight = own_mass * jnp.exp(own_peak - peak_all)
    pair_weight = jnp.where(
        in_use, pair_mass * jnp.exp(pair_peak - peak_all[:, None]), jnp.float32(0.0)
    )
    numerator = own_weight.transpose(0, 2, 1)[..., None] * own_mix + jnp.sum(
        pair_weight.transpose(0, 1, 3, 2)[..., None] * pair_mix, axis=1
    )
    denominator = (own_weight + jnp.sum(pair_weight, axis=1)).transpose(0, 2, 1)[..., None]
    attention = (numerator / denominator).astype(jnp.bfloat16).reshape(QROWS, head_cols)
    partial_value = jnp.dot(attention, out_weight, preferred_element_type=jnp.float32)
    piece_rows = QROWS // ctx_size
    summed = lax.psum_scatter(
        partial_value.astype(jnp.bfloat16), "tp", scatter_dimension=1, tiled=True
    )
    pieces = jnp.take(summed.reshape(ctx_size, piece_rows, summed.shape[1]), shard_order, axis=0)
    arrived = lax.all_to_all(pieces, "ctx", split_axis=0, concat_axis=0, tiled=True)
    return arrived.reshape(QROWS, summed.shape[1])


def solution(mesh):
    placed = (P("ctx", "tp"), P("ctx", "tp"), P("ctx", "tp"), P("tp", None), P("ctx", None), P())
    return jax.shard_map(
        local, mesh=mesh, in_specs=placed, out_specs=P("ctx", "tp"), check_vma=False
    )
```

profile of v0, /device:TPU:8, one launch (start us, length us, event | category | flops | bytes accessed | tf_op | source)
XLA Modules:
  0.0 320.3 jit_solution(15594569312614591931)
XLA Ops:
  6.5 0.8 copy.61
  9.3 1.1 reshape.264
  10.9 1.3 copy.84
  12.2 10.1 %all-to-all-start = ((bf16[32,2,16,512]{3,2,1,0:T(8,128)(2,1)}), bf16[32,2,16,512]{3,2,1,0:T(8,128)(2,1)S(1)}, u32[]{:S(2)}, u32[]{:S(2)}) async-start(bf16[32,2,16,512]{3,2,1,0:T(8,128)(2,1)} %bitcast.48), calls=%async_computation | async-start | bytes 2097152 | tf_op jit(solution)/shard_map/all_to_all | solution.py:89
  22.3 1.0 reshape.258
  23.4 26.2 %all-to-all-done = bf16[32,2,16,512]{3,2,1,0:T(8,128)(2,1)S(1)} async-done(((bf16[32,2,16,512]{3,2,1,0:T(8,128)(2,1)}), bf16[32,2,16,512]{3,2,1,0:T(8,128)(2,1)S(1)}, u32[]{:S(2)}, u32[]{:S(2)}) %all-to-all-start) | async-done | bytes 1048608 | tf_op jit(solution)/shard_map/all_to_all | solution.py:89
  49.9 49.6 %while.14 = (s32[]{:T(128)}, f32[8,8,16,512]{3,2,1,0:T(8,128)}, f32[8,8,4,16]{3,1,0,2:T(8,128)}, f32[8,8,4,16]{3,1,0,2:T(8,128)S(1)}, bf16[8,8,16,1,4,128]{5,4,2...) while((s32[]{:T(128)}, f32[8,8,16,512]{3,2,1,0:T(8,128)}, ...), condition=%wide.region_7.8_spmd, body=%wide.region_4.7_spmd.sunk | while | flops 1090583552 | bytes 34031748 | solution.py:104
  50.0 1.3 multiply_reduce_fusion.3
  51.3 1.5 fusion.56
  52.8 1.5 fusion.57
  56.2 1.3 multiply_reduce_fusion.3
  57.5 1.5 fusion.56
  59.0 1.5 fusion.57
  62.4 1.3 multiply_reduce_fusion.3
  63.7 1.5 fusion.56
  65.2 1.5 fusion.57
  68.5 1.3 multiply_reduce_fusion.3
  69.9 1.5 fusion.56
  71.4 1.5 fusion.57
  74.7 1.3 multiply_reduce_fusion.3
  76.1 1.5 fusion.56
  77.6 1.5 fusion.57
  81.0 1.3 multiply_reduce_fusion.3
  82.3 1.5 fusion.56
  83.8 1.5 fusion.57
  87.2 1.3 multiply_reduce_fusion.3
  88.5 1.5 fusion.56
  90.0 1.5 fusion.57
  93.4 1.3 multiply_reduce_fusion.3
  94.7 1.5 fusion.56
  96.2 1.5 fusion.57
  99.5 0.8 reshape.317
  100.3 5.2 %all-to-all-start.2 = ((f32[32,1,128]{2,1,0:T(1,128)}), f32[32,1,128]{2,1,0:T(1,128)S(1)}, u32[]{:S(2)}, u32[]{:S(2)}) async-start(f32[32,1,128]{2,1,0:T(1,128)} %reshape.317), calls=%async_computation.2 | async-start | bytes 32768 | tf_op jit(solution)/shard_map/all_to_all | solution.py:119
  105.5 7.4 %fusion.10 = (f32[1024]{0:T(1024)S(1)}, f32[1024,4096]{1,0:T(8,128)}) fusion(s32[1024]{0:T(1024)S(1)} %fusion.25, bf16[1024,128]{1,0:T(8,128)(2,1)S(1)} %bitcast.161, bf16[4096,128]{1,0:T(8,128)(2,1)S(1)} %get-tuple-element.176), kind=kOutput, calls=%fused_computation.20 | convolution fusion | flops 1090518016 | bytes 18096128 | tf_op jit(solution)/shard_map/jrd,kjd->jrk/dot_general | solution.py:23
  113.0 0.8 reshape.319
  113.8 8.3 %all-to-all-start.1 = ((f32[32,1,128]{2,1,0:T(1,128)}), f32[32,1,128]{2,1,0:T(1,128)S(1)}, u32[]{:S(2)}, u32[]{:S(2)}) async-start(f32[32,1,128]{2,1,0:T(1,128)} %reshape.319), calls=%async_computation.1 | async-start | bytes 32768 | tf_op jit(solution)/shard_map/all_to_all | solution.py:112
  122.4 6.8 %all-to-all-done.1 = f32[32,1,128]{2,1,0:T(1,128)S(1)} async-done(((f32[32,1,128]{2,1,0:T(1,128)}), f32[32,1,128]{2,1,0:T(1,128)S(1)}, u32[]{:S(2)}, u32[]{:S(2)}) %all-to-all-start.1) | async-done | bytes 16416 | tf_op jit(solution)/shard_map/all_to_all | solution.py:112
  129.2 5.3 %all-to-all-start.3 = ((f32[32,2,16,512]{3,2,1,0:T(8,128)}), f32[32,2,16,512]{3,2,1,0:T(8,128)S(1)}, u32[]{:S(2)}, u32[]{:S(2)}) async-start(f32[32,2,16,512]{3,2,1,0:T(8,128)} %bitcast.143), calls=%async_computation.3 | async-start | bytes 4194304 | tf_op jit(solution)/shard_map/all_to_all | solution.py:105
  134.7 8.3 %fusion.9 = f32[1024]{0:T(1024)S(1)} fusion(f32[1024,4096]{1,0:T(8,128)} %get-tuple-element.99, f32[1024]{0:T(1024)S(1)} %get-tuple-element.98, s32[1024]{0:T(1024)S(1)} %fusion.25), kind=kLoop, calls=%fused_computation.19 | loop fusion | flops 20970496 | bytes 16789504 | tf_op jit(solution)/shard_map/reduce_sum | solution.py:30
  143.1 8.3 %fusion.13 = f32[1024,128]{1,0:T(8,128)S(1)} fusion(bf16[4096,128]{1,0:T(8,128)(2,1)} %get-tuple-element.186, f32[1024,4096]{1,0:T(8,128)} %get-tuple-element.99, f32[1024]{0:T(1024)S(1)} %get-tuple-element.98, s32[1024]{0:T(1024)S(1)} %fusion.25, f32[1024]{0:T(1024)S(1)} %fusion.9), kind=kOutput, calls=%fused_computation.25 | convolution fusion | flops 1094844416 | bytes 18362368 | tf_op jit(solution)/shard_map/jrk,kjd->jrd/dot_general | solution.py:31
  156.7 26.9 %all-to-all-done.3 = f32[32,2,16,512]{3,2,1,0:T(8,128)S(1)} async-done(((f32[32,2,16,512]{3,2,1,0:T(8,128)}), f32[32,2,16,512]{3,2,1,0:T(8,128)S(1)}, u32[]{:S(2)}, u32[]{:S(2)}) %all-to-all-start.3) | async-done | bytes 2097184 | tf_op jit(solution)/shard_map/all_to_all | solution.py:105
  183.6 1.8 gather_fusion
  185.4 1.8 gather.14
  187.2 1.2 multiply_reduce_fusion.1
  189.1 7.7 %convolution_convert_fusion = bf16[256,8192]{1,0:T(8,128)(2,1)} fusion(bf16[512,8192]{1,0:T(8,128)(2,1)} %param.13, f32[32,8,4,128]{3,2,1,0:T(4,128)S(1)} %bitcast.148, f32[32,8,4,128]{3,2,1,0:T(4,128)S(1)} %bitcast.157, f32[32,8,4,128]{3,2,1,0:T(4,128)S(1)} %bitcast.150, f32[32,8,4,128]{3,2,1,0:T(4,128)S(1)} %bitcast.149), kind=kOutput, calls=%fused_computation.21 | convolution fusion | flops 2150105088 | bytes 14680064 | tf_op jit(solution)/shard_map/dot_general | solution.py:146
  196.9 88.5 %reduce-scatter.2.cloned.1.call-done = bf16[256,1024]{1,0:T(8,128)(2,1)} async-done(((bf16[256,8192]{1,0:T(8,128)(2,1)}), bf16[256,1024]{1,0:T(8,128)(2,1)}) %reduce-scatter.2.cloned.1.call-update) | async-done | bytes 524304 | tf_op jit(solution)/shard_map/reduce_scatter | solution.py:148
  285.3 1.6 gather_fusion.1
  287.1 25.6 %all_to_all.25 = bf16[32,8,1024]{2,1,0:T(8,128)(2,1)S(1)} all-to-all(bf16[32,8,1024]{2,1,0:T(8,128)(2,1)S(1)} %broadcast_select_fusion), channel_id=1, replica_groups=mesh['ctx'=32,'tp'=8] {'ctx'}, dimensions={0} | all-to-all | bytes 1048576 | tf_op jit(solution)/shard_map/all_to_all | solution.py:152
  (150 shorter events, 25.0 us)
Async XLA Ops:
  6.5 43.3 %copy-start = (bf16[4096,128]{1,0:T(8,128)(2,1)S(1)}, bf16[4096,128]{1,0:T(8,128)(2,1)}, u32[]{:S(2)}) copy-start(bf16[4096,128]{1,0:T(8,128)(2,1)} %param.11) | copy-start | bytes 3145732
  7.5 0.5 copy-start.2
  8.0 0.5 copy-start.4
  12.2 37.4 %all-to-all-start = ((bf16[32,2,16,512]{3,2,1,0:T(8,128)(2,1)}), bf16[32,2,16,512]{3,2,1,0:T(8,128)(2,1)S(1)}, u32[]{:S(2)}, u32[]{:S(2)}) async-start(bf16[32,2,16,512]{3,2,1,0:T(8,128)(2,1)} %bitcast.48), calls=%async_computation | async-start | bytes 2097152 | tf_op jit(solution)/shard_map/all_to_all | solution.py:89
  50.0 2.9 copy-start.7
  56.2 2.9 copy-start.7
  62.3 2.9 copy-start.7
  68.5 2.9 copy-start.7
  74.7 2.9 copy-start.7
  80.9 2.9 copy-start.7
  87.1 2.9 copy-start.7
  93.3 2.9 copy-start.7
  100.3 13.5 %all-to-all-start.2 = ((f32[32,1,128]{2,1,0:T(1,128)}), f32[32,1,128]{2,1,0:T(1,128)S(1)}, u32[]{:S(2)}, u32[]{:S(2)}) async-start(f32[32,1,128]{2,1,0:T(1,128)} %reshape.317), calls=%async_computation.2 | async-start | bytes 32768 | tf_op jit(solution)/shard_map/all_to_all | solution.py:119
  105.5 7.5 %copy-start.1 = (f32[8,8,4,16]{3,1,0,2:T(8,128)S(1)}, f32[8,8,4,16]{3,1,0,2:T(8,128)}, u32[]{:S(2)}) copy-start(f32[8,8,4,16]{3,1,0,2:T(8,128)} %get-tuple-element.45) | copy-start | bytes 49156
  113.8 15.4 %all-to-all-start.1 = ((f32[32,1,128]{2,1,0:T(1,128)}), f32[32,1,128]{2,1,0:T(1,128)S(1)}, u32[]{:S(2)}, u32[]{:S(2)}) async-start(f32[32,1,128]{2,1,0:T(1,128)} %reshape.319), calls=%async_computation.1 | async-start | bytes 32768 | tf_op jit(solution)/shard_map/all_to_all | solution.py:112
  129.2 54.4 %all-to-all-start.3 = ((f32[32,2,16,512]{3,2,1,0:T(8,128)}), f32[32,2,16,512]{3,2,1,0:T(8,128)S(1)}, u32[]{:S(2)}, u32[]{:S(2)}) async-start(f32[32,2,16,512]{3,2,1,0:T(8,128)} %bitcast.143), calls=%async_computation.3 | async-start | bytes 4194304 | tf_op jit(solution)/shard_map/all_to_all | solution.py:105
  134.4 150.9 %reduce-scatter.2.cloned.1.call-start = ((), (), s32[]{:S(2)}) async-start(), calls=%async_computation.6 | async-start | bytes 4718592 | tf_op jit(solution)/shard_map/reduce_scatter | solution.py:148
  143.0 8.7 %copy-start.3 = (s32[48]{0:T(128)S(1)}, s32[48]{0:T(128)}, u32[]{:S(2)}) copy-start(s32[48]{0:T(128)} %copy-done.2) | copy-start | bytes 580
  143.0 8.7 %copy-start.5 = (s32[48]{0:T(128)S(1)}, s32[48]{0:T(128)}, u32[]{:S(2)}) copy-start(s32[48]{0:T(128)} %copy-done.4) | copy-start | bytes 580
  151.4 35.8 %copy-start.6 = (pred[16,3]{1,0:T(8,128)(4,1)S(1)}, pred[16,3]{1,0:T(8,128)(4,1)}, u32[]{:S(2)}) copy-start(pred[16,3]{1,0:T(8,128)(4,1)} %get-tuple-element.83) | copy-start | bytes 148
  189.1 7.8 %copy-start.8 = (s32[32]{0:T(128)S(1)}, s32[32]{0:T(128)}, u32[]{:S(2)}) copy-start(s32[32]{0:T(128)} %param.15) | copy-start | bytes 388
Sparse Core Ops, SparseCore 0:
  196.9 88.3 reduce-scatter.1
where the time goes:
time: 322 us; the launch traced here: 320 us
  waiting for transfers between devices  148 us (46%)
  matrix products  46.2 us (14%)
  local copies, waits for them, and re-layouts  32.5 us (10%)
  starting transfers between devices  29.1 us (9%)
  blocking collectives  25.6 us (8%)
  other arithmetic  24.4 us (8%)
  between operations  13.8 us (4%)
    reduce_scatter x1, waiting for transfers between devices, local(): lax.psum_scatter(partial_value.astype(jnp.bfloat16), 'tp', scatter_dimens...  88.5 us
    all_to_all x1, waiting for transfers between devices, local(): lax.all_to_all(results[0].reshape(sources, item_count, TILE, head_cols),...  26.9 us
    all_to_all x1, waiting for transfers between devices, local(): lax.all_to_all(outgoing, 'ctx', split_axis=0, concat_axis=0, tiled=True)  26.2 us
    all_to_all x1, blocking collectives, local(): lax.all_to_all(pieces, 'ctx', split_axis=0, concat_axis=0, tiled=True)  25.6 us
    reduce_sum x9, other arithmetic, attend(): row_mass = jnp.sum(weights, axis=-1)  20.4 us
    dot_general x9, matrix products, attend(): jnp.einsum('jrk,kjd->jrd', weights.astype(jnp.bfloat16), value_rows, pref...  20 us
    dot_general x9, matrix products, attend(): jnp.einsum('jrd,kjd->jrk', query_rows, key_rows, preferred_element_type=j...  18.1 us
    dynamic_update_slice x16, local copies, waits for them, and re-layouts, local(): results = lax.map(serve_group, batches)  10.8 us
  transfers between devices with their start and end apart: 5, of which 4 were waited for; matrix products, arithmetic and copies ran while one was open for 10% of the time, Pallas kernels for 0%

commit v1 on v0

v1 whole, which is shorter than its diff:
```python
import functools
import math

import jax
import jax.numpy as jnp
from jax import lax
from jax.experimental import pallas as pl
from jax.experimental.pallas import tpu as pltpu
from jax.sharding import PartitionSpec as P

DH = 128
TOPK = 3
TILE = 16
CAP = 2
KEYS = 256
UNIT = 4
SCALE = math.log2(math.e) / math.sqrt(DH)
MESH = pl.DeviceIdType.MESH
BF = jnp.bfloat16
F32 = jnp.float32


def iota(shape, dim):
    return lax.broadcasted_iota(jnp.int32, shape, dim)


def dot(a, b):
    return jnp.dot(a, b, preferred_element_type=F32)


def dot_nt(a, b):
    return lax.dot_general(a, b, (((1,), (1,)), ((), ())), preferred_element_type=F32)


def attend(rows, kt, vx, masked):
    count = rows.shape[0]
    scaled = rows.astype(F32) * SCALE
    high = scaled.astype(BF)
    low = (scaled - high.astype(F32)).astype(BF)
    rows = jnp.concatenate([high, low], axis=1)
    steps = vx.shape[0] // KEYS
    peak, total = None, None
    for step in range(steps):
        keys = pl.ds(step * KEYS, KEYS)
        scores = dot(rows, kt[:, keys])
        if masked and step == steps - 1:
            shape = (count, KEYS)
            scores = jnp.where(iota(shape, 1) <= iota(shape, 0) % KEYS, scores, -1e30)
        top = jnp.max(scores, axis=1, keepdims=True)
        if peak is not None:
            top = jnp.maximum(top, peak)
        term = dot(jnp.exp2(scores - top).astype(BF), vx[keys, :])
        total = term if peak is None else total * jnp.exp2(peak - top) + term
        peak = top
    mass = total[:, DH:]
    return total[:, :DH] / mass, peak + jnp.log2(mass)


def kernel(
    n, nt,
    q_ref, sel_ref, order_ref, k_ref, v_ref, w_ref, out_ref,
    kraw, kt, vx, outq, recvq, ret, back, pick, perm, own_mix, own_log,
    wfull, pieces, arrived, ag, acc,
    load_sem, qs_sem, qr_sem, bs_sem, br_sem, ws_sem, wr_sem, fs_sem, fr_sem,
    ts_sem, tr_sem, as_sem, ar_sem,
):
    c = lax.axis_index("ctx")
    t = lax.axis_index("tp")
    core = lax.rem(c, 2)
    sibling = c + 1 - 2 * core
    heads = q_ref.shape[1] // DH
    tiles = sel_ref.shape[0]
    rows = q_ref.shape[0]
    slots = n * CAP
    pair_rows = CAP * TILE
    slot_rows = n * pair_rows
    piece = rows // n
    cols = out_ref.shape[1]
    depth = w_ref.shape[0]
    half = depth // 2

    barrier = pltpu.get_barrier_semaphore()

    def greet_ctx(j, carry):
        pl.semaphore_signal(
            barrier, inc=1, device_id=(lax.rem(c + j, n), t), device_id_type=MESH
        )
        return carry

    lax.fori_loop(1, n, greet_ctx, 0)

    def greet_tp(j, carry):
        pl.semaphore_signal(
            barrier, inc=1, device_id=(c, lax.rem(t + j, nt)), device_id_type=MESH
        )
        return carry

    lax.fori_loop(1, nt, greet_tp, 0)

    load_k = pltpu.make_async_copy(k_ref, kraw, load_sem.at[0])
    load_v = pltpu.make_async_copy(v_ref, vx.at[:, pl.ds(0, DH)], load_sem.at[1])
    load_w = pltpu.make_async_copy(
        w_ref.at[:, pl.ds(pl.multiple_of(t * cols, cols), cols)], wfull.at[t], load_sem.at[2]
    )
    load_k.start()
    load_v.start()
    load_w.start()

    slot_shape = (tiles, slots)
    lane = iota(slot_shape, 1)
    chosen = [sel_ref[:, r : r + 1] for r in range(TOPK)]
    named = [(lane // CAP == chosen[r]) for r in range(TOPK)]
    hit = (named[0] | named[1] | named[2]).astype(F32)
    lower = (iota((tiles, tiles), 1) < iota((tiles, tiles), 0)).astype(BF)
    rank = dot(lower, hit.astype(BF))
    right_rank = (rank == (lane % CAP).astype(F32)).astype(F32)
    owner = (hit * right_rank).astype(BF)
    spread = (iota((tiles, rows), 1) // TILE == iota((tiles, rows), 0)).astype(BF)
    block = 256

    def fill(j, carry):
        base = pl.multiple_of(j * block, block)
        row = base + iota((block, slots), 0)
        of_slot = (row // TILE == iota((block, slots), 1)).astype(BF)
        of_tile = dot_nt(of_slot, owner).astype(BF)
        same = iota((block, rows), 0) % TILE == iota((block, rows), 1) % TILE
        gate = jnp.where(same, dot(of_tile, spread), 0.0).astype(BF)
        outq[pl.ds(base, block), :] = dot(gate, q_ref[...]).astype(BF)
        return carry

    lax.fori_loop(0, slot_rows // block, fill, 0)

    pl.semaphore_wait(barrier, n - 1 + nt - 1)

    def dispatch(k, s, peer=None):
        return pltpu.make_async_remote_copy(
            src_ref=outq.at[pl.ds(pl.multiple_of(k * pair_rows, pair_rows), pair_rows), :],
            dst_ref=recvq.at[s],
            send_sem=qs_sem.at[k],
            recv_sem=qr_sem.at[s],
            device_id=(k if peer is None else peer, t),
            device_id_type=MESH,
        )

    def send_queries(j, carry):
        dispatch(c - 1 - j, c).start()
        return carry

    lax.fori_loop(0, c, send_queries, 0)

    def weight_copy(dest, j):
        return pltpu.make_async_remote_copy(
            src_ref=w_ref.at[
                pl.ds(pl.multiple_of(core * half, half), half),
                pl.ds(pl.multiple_of(dest * cols, cols), cols),
            ],
            dst_ref=wfull.at[t, pl.ds(pl.multiple_of(core * half, half), half), :],
            send_sem=ws_sem.at[j],
            recv_sem=wr_sem.at[j],
            device_id=(c, dest),
            device_id_type=MESH,
        )

    def weight_arrival(source, j):
        view = wfull.at[source, pl.ds(pl.multiple_of(core * half, half), half), :]
        return pltpu.make_async_remote_copy(
            src_ref=view,
            dst_ref=view,
            send_sem=ws_sem.at[j],
            recv_sem=wr_sem.at[j],
            device_id=(c, source),
            device_id_type=MESH,
        )

    def weight_share(source, j, which):
        view = wfull.at[source, pl.ds(pl.multiple_of(which * half, half), half), :]
        return pltpu.make_async_remote_copy(
            src_ref=view,
            dst_ref=view,
            send_sem=fs_sem.at[j],
            recv_sem=fr_sem.at[j],
            device_id=(sibling, t),
            device_id_type=MESH,
        )

    def send_weights(j, carry):
        weight_copy(lax.rem(t + j, nt), j).start()
        return carry

    lax.fori_loop(1, nt, send_weights, 0)

    recvq[c] = jnp.zeros(recvq.shape[1:], BF)

    def clear(k, carry):
        back[pl.ds(pl.multiple_of(k * pair_rows, pair_rows), pair_rows), :] = jnp.zeros(
            (pair_rows, back.shape[1]), BF
        )
        return carry

    lax.fori_loop(c, n, clear, 0)

    load_k.wait()
    kt[0:DH, :] = kraw[...].T
    kt[DH:, :] = kt[0:DH, :]
    load_v.wait()
    vx[:, DH:] = jnp.ones((vx.shape[0], DH), BF)

    for first in range(0, heads, 2):
        pair = jnp.concatenate(
            [q_ref[:, h * DH : (h + 1) * DH] for h in (first, first + 1)], axis=0
        )
        mix, log_mass = attend(pair, kt, vx, True)
        for i, h in enumerate((first, first + 1)):
            own_mix[:, h * DH : (h + 1) * DH] = mix[i * rows : (i + 1) * rows]
            own_log[:, h * DH : (h + 1) * DH] = log_mass[i * rows : (i + 1) * rows]

    def give_back(s, k, peer=None):
        return pltpu.make_async_remote_copy(
            src_ref=ret.at[s],
            dst_ref=back.at[pl.ds(pl.multiple_of(k * pair_rows, pair_rows), pair_rows), :],
            send_sem=bs_sem.at[s],
            recv_sem=br_sem.at[k],
            device_id=(s if peer is None else peer, t),
            device_id_type=MESH,
        )

    def serve(g, carry):
        names = []
        for u in range(UNIT):
            s = c + 1 + g * UNIT + u
            names.append((s, jnp.where(s < n, s, c)))

            @pl.when(s < n)
            def _():
                dispatch(c, s, s).wait_recv()

        parts = []
        for s, at in names:
            held = recvq[at]
            parts += [held[:, h * DH : (h + 1) * DH] for h in range(heads)]
        mix, log_mass = attend(jnp.concatenate(parts, axis=0), kt, vx, False)
        spot = iota((pair_rows, DH), 1)
        for u, (s, at) in enumerate(names):
            base = u * heads * pair_rows
            stat = jnp.zeros((pair_rows, DH), F32)
            for h in range(heads):
                here = slice(base + h * pair_rows, base + (h + 1) * pair_rows)
                ret[at, :, h * DH : (h + 1) * DH] = mix[here].astype(BF)
                stat = jnp.where(spot % heads == h, log_mass[here], stat)
            high = stat.astype(BF).astype(F32)
            middle = (stat - high).astype(BF).astype(F32)
            low = stat - high - middle
            packed = jnp.where(spot < heads, high, jnp.where(spot < 2 * heads, middle, low))
            packed = jnp.where(spot < 3 * heads, packed, 0.0)
            ret[at, :, heads * DH :] = packed.astype(BF)

            @pl.when(s < n)
            def _():
                give_back(s, c).start()

        return carry

    lax.fori_loop(0, (n - 1 - c + UNIT - 1) // UNIT, serve, 0)

    for r in range(TOPK):
        mine = (named[r].astype(F32) * right_rank).astype(BF)
        of_row = dot(
            (iota((rows, tiles), 0) // TILE == iota((rows, tiles), 1)).astype(BF), mine
        ).astype(BF)
        to_slot = (iota((slots, slot_rows), 1) // TILE == iota((slots, slot_rows), 0)).astype(BF)
        same = iota((rows, slot_rows), 0) % TILE == iota((rows, slot_rows), 1) % TILE
        pick[r] = jnp.where(same, dot(of_row, to_slot), 0.0).astype(BF)
    wanted = (iota((n, n), 0) == order_ref[...]).astype(BF)
    row2 = iota((2 * rows, n), 0)
    of_shard = (row2 // (2 * piece) == iota((2 * rows, n), 1)).astype(BF)
    of_piece = dot_nt(of_shard, wanted).astype(BF)
    to_rows = (iota((n, rows), 1) // piece == iota((n, rows), 0)).astype(BF)
    same = iota((2 * rows, rows), 0) % piece == iota((2 * rows, rows), 1) % piece
    perm[...] = jnp.where(same, dot(of_piece, to_rows), 0.0).astype(BF)

    def share(j, carry):
        source = lax.rem(t + nt - j, nt)
        weight_arrival(source, j).wait_recv()
        weight_share(source, j, core).start()
        return carry

    lax.fori_loop(1, nt, share, 0)

    def await_back(j, carry):
        give_back(c, c - 1 - j, c - 1 - j).wait_recv()
        return carry

    lax.fori_loop(0, c, await_back, 0)
    to_heads = (
        (iota((DH, heads * DH), 0) % heads == iota((DH, heads * DH), 1) // DH)
        & (iota((DH, heads * DH), 0) < 3 * heads)
    ).astype(BF)
    row_of = (iota((rows, tiles), 0) // TILE == iota((rows, tiles), 1)).astype(BF)
    logs, mixes = [own_log[...]], [own_mix[...]]
    for r in range(TOPK):
        taken = dot(pick[r], back[...])
        live = dot(row_of, jnp.broadcast_to((chosen[r] >= 0).astype(F32), (tiles, heads * DH)).astype(BF))
        log_mass = dot(taken[:, heads * DH :].astype(BF), to_heads)
        logs.append(jnp.where(live > 0.5, log_mass, -1e30))
        mixes.append(taken[:, : heads * DH])
    top = jnp.maximum(jnp.maximum(logs[0], logs[1]), jnp.maximum(logs[2], logs[3]))
    numerator, denominator = 0.0, 0.0
    for log_mass, mix in zip(logs, mixes):
        weight = jnp.exp2(log_mass - top)
        numerator = numerator + weight * mix
        denominator = denominator + weight
    attention = (numerator / denominator).astype(BF)

    mid = heads * DH // 2
    left = dot(perm[...], attention[:, :mid])
    right = dot(perm[...], attention[:, mid:])
    side = iota((2 * rows, mid), 0) // piece % 2
    pieces[...] = jnp.where(side == 0, left, right).astype(BF)
    size = 2 * piece

    def deliver(d, s):
        return pltpu.make_async_remote_copy(
            src_ref=pieces.at[pl.ds(pl.multiple_of(d * size, size), size), :],
            dst_ref=arrived.at[pl.ds(pl.multiple_of(s * size, size), size), :],
            send_sem=ts_sem.at[d],
            recv_sem=tr_sem.at[s],
            device_id=(d, t),
            device_id_type=MESH,
        )

    def send_piece(j, carry):
        deliver(lax.rem(c + j, n), c).start()
        return carry

    lax.fori_loop(1, n, send_piece, 0)
    here = pl.ds(pl.multiple_of(c * size, size), size)
    arrived[here, :] = pieces[here, :]

    def await_piece(j, carry):
        s = lax.rem(c + n - j, n)
        pltpu.make_async_remote_copy(
            src_ref=arrived.at[pl.ds(pl.multiple_of(s * size, size), size), :],
            dst_ref=arrived.at[pl.ds(pl.multiple_of(s * size, size), size), :],
            send_sem=ts_sem.at[s],
            recv_sem=tr_sem.at[s],
            device_id=(s, t),
            device_id_type=MESH,
        ).wait_recv()
        return carry

    lax.fori_loop(1, n, await_piece, 0)
    split = arrived[...].astype(F32).reshape(n, 2, piece, mid)
    ag[t, :, :mid] = split[:, 0].reshape(rows, mid).astype(BF)
    ag[t, :, mid:] = split[:, 1].reshape(rows, mid).astype(BF)

    ring = nt // 2
    x, y = t // 2, lax.rem(t, 2)
    after, before, across = lax.rem(x + 1, ring), lax.rem(x + ring - 1, ring), 1 - y
    opposite = lax.rem(x + 2, ring)
    middle_row = rows // 2

    def tp_copy(which, part, dest, send, recv):
        if part is None:
            view = ag.at[which]
        else:
            view = ag.at[which, pl.ds(part * middle_row, middle_row), :]
        return pltpu.make_async_remote_copy(
            src_ref=view,
            dst_ref=view,
            send_sem=as_sem.at[send],
            recv_sem=ar_sem.at[which, recv],
            device_id=(c, dest),
            device_id_type=MESH,
        )

    sent = []

    def start(*spec):
        copy = tp_copy(*spec)
        copy.start()
        sent.append(copy)

    def project(which, first=False):
        term = dot(ag[which], wfull[which])
        acc[...] = term if first else acc[...] + term

    start(t, None, after * 2 + y, 0, 0)
    start(t, None, before * 2 + y, 1, 0)
    start(t, None, x * 2 + across, 2, 0)
    load_w.wait()

    def await_share(j, carry):
        weight_share(lax.rem(t + nt - j, nt), j, 1 - core).wait_recv()
        return carry

    lax.fori_loop(1, nt, await_share, 0)
    project(t, True)
    low, high, over = before * 2 + y, after * 2 + y, x * 2 + across
    tp_copy(low, None, low, 0, 0).wait_recv()
    start(low, 0, after * 2 + y, 3, 0)
    tp_copy(high, None, high, 0, 0).wait_recv()
    start(high, 1, before * 2 + y, 4, 1)
    tp_copy(over, None, over, 0, 0).wait_recv()
    start(over, None, after * 2 + y, 5, 0)
    start(over, None, before * 2 + y, 6, 0)
    project(low)
    project(high)
    project(over)
    low2, high2 = before * 2 + across, after * 2 + across
    tp_copy(low2, None, low, 0, 0).wait_recv()
    start(low2, 0, after * 2 + y, 7, 0)
    tp_copy(high2, None, high, 0, 0).wait_recv()
    start(high2, 1, before * 2 + y, 8, 1)
    far, far2 = opposite * 2 + y, opposite * 2 + across
    tp_copy(far, 0, low, 0, 0).wait_recv()
    tp_copy(far, 1, high, 0, 1).wait_recv()
    project(low2)
    project(high2)
    project(far)
    tp_copy(far2, 0, low, 0, 0).wait_recv()
    tp_copy(far2, 1, high, 0, 1).wait_recv()
    out_ref[...] = (acc[...] + dot(ag[far2], wfull[far2])).astype(BF)

    for copy in sent:
        copy.wait_send()

    def drain_ctx(j, carry):
        deliver(lax.rem(c + j, n), c).wait_send()
        return carry

    lax.fori_loop(1, n, drain_ctx, 0)

    def drain_queries(k, carry):
        dispatch(k, c).wait_send()
        return carry

    lax.fori_loop(0, c, drain_queries, 0)

    def drain_back(s, carry):
        give_back(s, c).wait_send()
        return carry

    lax.fori_loop(c + 1, n, drain_back, 0)

    def drain_weights(j, carry):
        weight_copy(lax.rem(t + j, nt), j).wait_send()
        weight_share(lax.rem(t + nt - j, nt), j, core).wait_send()
        return carry

    lax.fori_loop(1, nt, drain_weights, 0)


def local(queries, key_cache, values, out_weight, selected, shard_order):
    n, nt = lax.axis_size("ctx"), lax.axis_size("tp")
    rows, width = queries.shape
    keys = key_cache.shape[0]
    depth, model = out_weight.shape
    cols = model // nt
    pair_rows = CAP * TILE
    dma = pltpu.SemaphoreType.DMA
    vmem = pl.BlockSpec(memory_space=pltpu.VMEM)
    hbm = pl.BlockSpec(memory_space=pl.ANY)
    return pl.pallas_call(
        functools.partial(kernel, n, nt),
        out_shape=jax.ShapeDtypeStruct((rows, cols), BF),
        in_specs=[vmem, vmem, vmem, hbm, hbm, hbm],
        out_specs=vmem,
        scratch_shapes=[
            pltpu.VMEM((keys, DH), BF),
            pltpu.VMEM((2 * DH, keys), BF),
            pltpu.VMEM((keys, 2 * DH), BF),
            pltpu.VMEM((n * pair_rows, width), BF),
            pltpu.VMEM((n, pair_rows, width), BF),
            pltpu.VMEM((n, pair_rows, width + DH), BF),
            pltpu.VMEM((n * pair_rows, width + DH), BF),
            pltpu.VMEM((TOPK, rows, n * pair_rows), BF),
            pltpu.VMEM((2 * rows, rows), BF),
            pltpu.VMEM((rows, width), F32),
            pltpu.VMEM((rows, width), F32),
            pltpu.VMEM((nt, depth, cols), BF),
            pltpu.VMEM((2 * rows, width // 2), BF),
            pltpu.VMEM((2 * rows, width // 2), BF),
            pltpu.VMEM((nt, rows, width), BF),
            pltpu.VMEM((rows, cols), F32),
            dma((3,)), dma((n,)), dma((n,)), dma((n,)), dma((n,)),
            dma((nt,)), dma((nt,)), dma((nt,)), dma((nt,)),
            dma((n,)), dma((n,)), dma((9,)), dma((nt, 2)),
        ],
        compiler_params=pltpu.CompilerParams(
            collective_id=0, has_side_effects=True, vmem_limit_bytes=58 * 2**20
        ),
        name="sublayer",
    )(queries, selected, shard_order.reshape(1, n), key_cache, values, out_weight)


def solution(mesh):
    placed = (P("ctx", "tp"), P("ctx", "tp"), P("ctx", "tp"), P("tp", None), P("ctx", None), P())
    return jax.shard_map(
        local, mesh=mesh, in_specs=placed, out_specs=P("ctx", "tp"), check_vma=False
    )
```

time: 322 us -> 132 us (0.41)
  waiting for transfers between devices: 148 us -> 0 us
  Pallas kernels: 0 us -> 128 us
  matrix products: 46.2 us -> 0 us
  local copies, waits for them, and re-layouts: 32.5 us -> 3.22 us
  starting transfers between devices: 29.1 us -> 0 us
  blocking collectives: 25.6 us -> 0 us
  other arithmetic: 24.4 us -> 0 us
  between operations: 13.8 us -> 0.01 us
    pallas_call x0 -> x1, Pallas kernels: none -> 128 us  [local(): pl.pallas_call(functools.partial(kernel, n, nt), out_shape=jax.ShapeDtype...]
    reduce_scatter x1 -> x0, waiting for transfers between devices: 88.5 us -> none  [local(): lax.psum_scatter(partial_value.astype(jnp.bfloat16), 'tp', scatter_dimens...]
    all_to_all x4 -> x0, waiting for transfers between devices: 59.8 us -> none  [the longest x1 26.9 us: local(): lax.all_to_all(results[0].reshape(sources, item_count, TILE, head_cols),...]
    dot_general x20 -> x0, matrix products: 46.2 us -> none  [the longest x9 20 us: attend(): jnp.einsum('jrk,kjd->jrd', weights.astype(jnp.bfloat16), value_rows, pref...]
    all_to_all x4 -> x0, starting transfers between devices: 28.8 us -> none  [the longest x1 10.1 us: local(): lax.all_to_all(outgoing, 'ctx', split_axis=0, concat_axis=0, tiled=True)]
    all_to_all x1 -> x0, blocking collectives: 25.6 us -> none  [local(): lax.all_to_all(pieces, 'ctx', split_axis=0, concat_axis=0, tiled=True)]
    reduce_sum x12 -> x0, other arithmetic: 21.8 us -> none  [the longest x9 20.4 us: attend(): row_mass = jnp.sum(weights, axis=-1)]
    dynamic_update_slice x16 -> x0, local copies, waits for them, and re-layouts: 10.8 us -> none  [local(): results = lax.map(serve_group, batches)]
  transfers between devices with their start and end apart: 5 -> 0, of which waited for: 4 -> 0; matrix products, arithmetic and copies ran while one was open for 10% -> 0% of each run, Pallas kernels for 0% -> 0%
where the time goes in v1:
time: 132 us
  Pallas kernels  128 us (97%)
  local copies, waits for them, and re-layouts  3.22 us (2%)
    pallas_call x1, Pallas kernels, local(): pl.pallas_call(functools.partial(kernel, n, nt), out_shape=jax.ShapeDtype...  128 us
    unnamed x2, local copies, waits for them, and re-layouts  3.22 us

profile of v1, /device:TPU:8, one launch (start us, length us, event | category | flops | bytes accessed | tf_op | source)
XLA Modules:
  0.0 131.6 jit_solution(14241221379320438612)
XLA Ops:
  0.0 1.4 %copy.7.sel_ref = s32[16,3]{1,0:T(8,128)} copy(s32[16,3]{0,1:T(4,128)} %param.10) | data formatting | bytes 384 | tf_op args[4]
  1.4 128.4 %sublayer.1 = bf16[256,1024]{1,0:T(8,128)(2,1)} custom-call(bf16[256,512]{1,0:T(8,128)(2,1)} %q_ref.1, s32[16,3]{1,0:T(8,128)} %copy.7.sel_ref, s32[1,32]{1,0:T(1,128)} %bitcast.1, bf16[4096,128]{1,0:T(8,128)(2,1)} %k_ref.1, bf16[4096,128]{1,0:T(8,128)(2,1)} %v_ref.1, bf16[512,8192]{1,0:T(8,128)(2,1)} %w_ref.1), custom_call_target="tpu_custom_call" | custom-call | tf_op jit(solution)/shard_map/sublayer/pallas_call | solution.py:463
  129.7 1.9 %copy.9 = bf16[256,1024]{1,0:T(8,128)(2,1)} copy(bf16[256,1024]{1,0:T(8,128)(2,1)} %sublayer.1) | data formatting | bytes 1048576

commit v2 on v1

v2 whole, which is shorter than its diff:
```python
import functools
import math

import jax
import jax.numpy as jnp
from jax import lax
from jax.experimental import pallas as pl
from jax.experimental.pallas import tpu as pltpu
from jax.sharding import PartitionSpec as P

DH = 128
TOPK = 3
TILE = 16
CAP = 2
KEYS = 256
UNIT = 4
SCALE = math.log2(math.e) / math.sqrt(DH)
MESH = pl.DeviceIdType.MESH
BF = jnp.bfloat16
F32 = jnp.float32


def iota(shape, dim):
    return lax.broadcasted_iota(jnp.int32, shape, dim)


def dot(a, b):
    return jnp.dot(a, b, preferred_element_type=F32)


def dot_nt(a, b):
    return lax.dot_general(a, b, (((1,), (1,)), ((), ())), preferred_element_type=F32)


def attend(rows, kt, vx, masked):
    count = rows.shape[0]
    scaled = rows.astype(F32) * SCALE
    high = scaled.astype(BF)
    low = (scaled - high.astype(F32)).astype(BF)
    rows = jnp.concatenate([high, low], axis=1)
    steps = vx.shape[0] // KEYS
    peak, total = None, None
    for step in range(steps):
        keys = pl.ds(step * KEYS, KEYS)
        scores = dot(rows, kt[:, keys])
        if masked and step == steps - 1:
            shape = (count, KEYS)
            scores = jnp.where(iota(shape, 1) <= iota(shape, 0) % KEYS, scores, -1e30)
        top = jnp.max(scores, axis=1, keepdims=True)
        if peak is not None:
            top = jnp.maximum(top, peak)
        term = dot(jnp.exp2(scores - top).astype(BF), vx[keys, :])
        total = term if peak is None else total * jnp.exp2(peak - top) + term
        peak = top
    mass = total[:, DH:]
    return total[:, :DH] / mass, peak + jnp.log2(mass)


def kernel(
    n, nt,
    q_ref, sel_ref, order_ref, k_ref, v_ref, w_ref, out_ref,
    kraw, kt, vx, outq, recvq, ret, back, pick, perm, own_mix, own_log,
    wfull, pieces, arrived, ag, term_out, term_in, acc,
    load_sem, qs_sem, qr_sem, bs_sem, br_sem, ws_sem, wr_sem, fs_sem, fr_sem,
    ts_sem, tr_sem, ys_sem, yr_sem, xs_sem, xr_sem,
):
    c = lax.axis_index("ctx")
    t = lax.axis_index("tp")
    core = lax.rem(c, 2)
    sibling = c + 1 - 2 * core
    heads = q_ref.shape[1] // DH
    tiles = sel_ref.shape[1]
    rows = q_ref.shape[0]
    slots = n * CAP
    pair_rows = CAP * TILE
    slot_rows = n * pair_rows
    piece = rows // n
    cols = out_ref.shape[1]
    depth = w_ref.shape[0]
    half = depth // 2

    barrier = pltpu.get_barrier_semaphore()

    def greet_ctx(j, carry):
        pl.semaphore_signal(
            barrier, inc=1, device_id=(lax.rem(c + j, n), t), device_id_type=MESH
        )
        return carry

    lax.fori_loop(1, n, greet_ctx, 0)

    ring = nt // 2
    x, y = t // 2, lax.rem(t, 2)
    across = x * 2 + 1 - y

    def greet_x(j, carry):
        pl.semaphore_signal(
            barrier, inc=1, device_id=(c, lax.rem(x + j, ring) * 2 + y), device_id_type=MESH
        )
        return carry

    lax.fori_loop(1, ring, greet_x, 0)
    pl.semaphore_signal(barrier, inc=1, device_id=(c, across), device_id_type=MESH)

    load_k = pltpu.make_async_copy(k_ref, kraw, load_sem.at[0])
    load_v = pltpu.make_async_copy(v_ref, vx.at[:, pl.ds(0, DH)], load_sem.at[1])
    load_k.start()
    load_v.start()

    slot_shape = (tiles, slots)
    lane = iota(slot_shape, 1)
    square = (tiles, tiles)
    chosen = [
        jnp.sum(
            jnp.where(iota(square, 0) == iota(square, 1), sel_ref[r : r + 1, :].astype(F32), 0.0),
            axis=1,
            keepdims=True,
        ).astype(jnp.int32)
        for r in range(TOPK)
    ]
    named = [(lane // CAP == chosen[r]) for r in range(TOPK)]
    hit = (named[0] | named[1] | named[2]).astype(F32)
    lower = (iota((tiles, tiles), 1) < iota((tiles, tiles), 0)).astype(BF)
    rank = dot(lower, hit.astype(BF))
    right_rank = (rank == (lane % CAP).astype(F32)).astype(F32)
    owner = (hit * right_rank).astype(BF)
    spread = (iota((tiles, rows), 1) // TILE == iota((tiles, rows), 0)).astype(BF)
    block = 256

    def fill(j, carry):
        base = pl.multiple_of(j * block, block)
        row = base + iota((block, slots), 0)
        of_slot = (row // TILE == iota((block, slots), 1)).astype(BF)
        of_tile = dot_nt(of_slot, owner).astype(BF)
        same = iota((block, rows), 0) % TILE == iota((block, rows), 1) % TILE
        gate = jnp.where(same, dot(of_tile, spread), 0.0).astype(BF)
        outq[pl.ds(base, block), :] = dot(gate, q_ref[...]).astype(BF)
        return carry

    lax.fori_loop(0, slot_rows // block, fill, 0)

    pl.semaphore_wait(barrier, n - 1 + ring - 1 + 1)

    def dispatch(k, s, peer=None):
        return pltpu.make_async_remote_copy(
            src_ref=outq.at[pl.ds(pl.multiple_of(k * pair_rows, pair_rows), pair_rows), :],
            dst_ref=recvq.at[s],
            send_sem=qs_sem.at[k],
            recv_sem=qr_sem.at[s],
            device_id=(k if peer is None else peer, t),
            device_id_type=MESH,
        )

    def send_queries(j, carry):
        dispatch(j, c).start()
        return carry

    lax.fori_loop(0, c, send_queries, 0)

    def columns(dest):
        return pl.ds(pl.multiple_of(dest * 2 * cols, 2 * cols), 2 * cols)

    my_half = pl.ds(pl.multiple_of(core * half, half), half)
    its_half = pl.ds(pl.multiple_of((1 - core) * half, half), half)
    weight_load = pltpu.make_async_copy(w_ref.at[:, columns(x)], wfull.at[x], load_sem.at[2])
    weight_load.start()

    def weight_copy(dest):
        return pltpu.make_async_remote_copy(
            src_ref=w_ref.at[my_half, columns(dest)],
            dst_ref=wfull.at[x, my_half, :],
            send_sem=ws_sem.at[dest],
            recv_sem=wr_sem.at[x],
            device_id=(c, dest * 2 + y),
            device_id_type=MESH,
        )

    def weight_arrival(source):
        view = wfull.at[source, my_half, :]
        return pltpu.make_async_remote_copy(
            src_ref=view,
            dst_ref=view,
            send_sem=ws_sem.at[source],
            recv_sem=wr_sem.at[source],
            device_id=(c, source * 2 + y),
            device_id_type=MESH,
        )

    def weight_share(source, rows_of):
        view = wfull.at[source, rows_of, :]
        return pltpu.make_async_remote_copy(
            src_ref=view,
            dst_ref=view,
            send_sem=fs_sem.at[source],
            recv_sem=fr_sem.at[source],
            device_id=(sibling, t),
            device_id_type=MESH,
        )

    def send_weights(j, carry):
        weight_copy(lax.rem(x + j, ring)).start()
        return carry

    lax.fori_loop(1, ring, send_weights, 0)

    recvq[c] = jnp.zeros(recvq.shape[1:], BF)

    def clear(k, carry):
        back[k] = jnp.zeros(back.shape[1:], BF)
        return carry

    lax.fori_loop(c, n, clear, 0)

    for r in range(TOPK):
        mine = (named[r].astype(F32) * right_rank).astype(BF)
        of_row = dot(
            (iota((rows, tiles), 0) // TILE == iota((rows, tiles), 1)).astype(BF), mine
        ).astype(BF)
        to_slot = (iota((slots, slot_rows), 1) // TILE == iota((slots, slot_rows), 0)).astype(BF)
        same = iota((rows, slot_rows), 0) % TILE == iota((rows, slot_rows), 1) % TILE
        pick[r] = jnp.where(same, dot(of_row, to_slot), 0.0).astype(BF)
    wanted = (iota((n, n), 0) == order_ref[...]).astype(BF)
    row2 = iota((2 * rows, n), 0)
    of_shard = (row2 // (2 * piece) == iota((2 * rows, n), 1)).astype(BF)
    of_piece = dot_nt(of_shard, wanted).astype(BF)
    to_rows = (iota((n, rows), 1) // piece == iota((n, rows), 0)).astype(BF)
    same = iota((2 * rows, rows), 0) % piece == iota((2 * rows, rows), 1) % piece
    perm[...] = jnp.where(same, dot(of_piece, to_rows), 0.0).astype(BF)

    load_k.wait()
    kt[0:DH, :] = kraw[...].T
    kt[DH:, :] = kt[0:DH, :]
    load_v.wait()
    vx[:, DH:] = jnp.ones((vx.shape[0], DH), BF)

    for first in range(0, heads, 2):
        pair = jnp.concatenate(
            [q_ref[:, h * DH : (h + 1) * DH] for h in (first, first + 1)], axis=0
        )
        mix, log_mass = attend(pair, kt, vx, True)
        for i, h in enumerate((first, first + 1)):
            own_mix[:, h * DH : (h + 1) * DH] = mix[i * rows : (i + 1) * rows]
            own_log[:, h * DH : (h + 1) * DH] = log_mass[i * rows : (i + 1) * rows]

    def give_back(s, k, peer=None):
        return pltpu.make_async_remote_copy(
            src_ref=ret.at[s],
            dst_ref=back.at[k],
            send_sem=bs_sem.at[s],
            recv_sem=br_sem.at[k],
            device_id=(s if peer is None else peer, t),
            device_id_type=MESH,
        )

    def serve(g, carry):
        names = []
        for u in range(UNIT):
            s = c + 1 + g * UNIT + u
            names.append((s, jnp.where(s < n, s, c)))

            @pl.when(s < n)
            def _():
                dispatch(c, s, s).wait_recv()

        parts = []
        for s, at in names:
            held = recvq[at]
            parts += [held[:, h * DH : (h + 1) * DH] for h in range(heads)]
        mix, log_mass = attend(jnp.concatenate(parts, axis=0), kt, vx, False)
        spot = iota((TILE, DH), 1)
        for u, (s, at) in enumerate(names):
            base = u * heads * pair_rows
            ret[at, : heads * pair_rows, :] = mix[base : base + heads * pair_rows].astype(BF)
            stat = jnp.zeros((TILE, DH), F32)
            for i in range(CAP):
                for h in range(heads):
                    first = base + h * pair_rows + i * TILE
                    here = (spot // (3 * heads) == i) & (spot % heads == h)
                    stat = jnp.where(here, log_mass[first : first + TILE], stat)
            high = stat.astype(BF).astype(F32)
            middle = (stat - high).astype(BF).astype(F32)
            low = stat - high - middle
            part = spot % (3 * heads) // heads
            packed = jnp.where(part == 0, high, jnp.where(part == 1, middle, low))
            ret[at, heads * pair_rows :, :] = packed.astype(BF)

            @pl.when(s < n)
            def _():
                give_back(s, c).start()

        return carry

    groups = (n - 1 - c + UNIT - 1) // UNIT
    turn = jnp.minimum(groups, (c + 11) // UNIT)
    lax.fori_loop(0, turn, serve, 0)

    def await_back(j, carry):
        give_back(c, c - 1 - j, c - 1 - j).wait_recv()
        return carry

    lax.fori_loop(0, c, await_back, 0)
    to_heads = (
        (iota((DH, heads * DH), 0) % heads == iota((DH, heads * DH), 1) // DH)
        & (iota((DH, heads * DH), 0) < 3 * heads * CAP)
    ).astype(BF)
    row_of = (iota((rows, tiles), 0) // TILE == iota((rows, tiles), 1)).astype(BF)
    stats = back[:, heads * pair_rows :, :]
    stat_lane = iota(stats.shape, 2) // (3 * heads)
    stats = jnp.concatenate(
        [jnp.where(stat_lane == i, stats.astype(F32), 0.0).astype(BF) for i in range(CAP)], axis=1
    ).reshape(slot_rows, DH)
    logs, mixes = [own_log[...]], [own_mix[...]]
    for r in range(TOPK):
        live = dot(row_of, jnp.broadcast_to((chosen[r] >= 0).astype(F32), (tiles, heads * DH)).astype(BF))
        log_mass = dot(dot(pick[r], stats).astype(BF), to_heads)
        logs.append(jnp.where(live > 0.5, log_mass, -1e30))
        mixes.append(
            jnp.concatenate(
                [
                    dot(
                        pick[r],
                        back[:, h * pair_rows : (h + 1) * pair_rows, :].reshape(slot_rows, DH),
                    )
                    for h in range(heads)
                ],
                axis=1,
            )
        )
    top = jnp.maximum(jnp.maximum(logs[0], logs[1]), jnp.maximum(logs[2], logs[3]))
    numerator, denominator = 0.0, 0.0
    for log_mass, mix in zip(logs, mixes):
        weight = jnp.exp2(log_mass - top)
        numerator = numerator + weight * mix
        denominator = denominator + weight
    attention = (numerator / denominator).astype(BF)

    mid = heads * DH // 2
    left = dot(perm[...], attention[:, :mid])
    right = dot(perm[...], attention[:, mid:])
    side = iota((2 * rows, mid), 0) // piece % 2
    pieces[...] = jnp.where(side == 0, left, right).astype(BF)
    size = 2 * piece

    def deliver(d, s):
        return pltpu.make_async_remote_copy(
            src_ref=pieces.at[pl.ds(pl.multiple_of(d * size, size), size), :],
            dst_ref=arrived.at[pl.ds(pl.multiple_of(s * size, size), size), :],
            send_sem=ts_sem.at[d],
            recv_sem=tr_sem.at[s],
            device_id=(d, t),
            device_id_type=MESH,
        )

    def send_piece(j, carry):
        deliver(lax.rem(c + j, n), c).start()
        return carry

    lax.fori_loop(1, n, send_piece, 0)
    here = pl.ds(pl.multiple_of(c * size, size), size)
    arrived[here, :] = pieces[here, :]

    lax.fori_loop(turn, groups, serve, 0)

    def share(j, carry):
        source = lax.rem(x + j, ring)
        weight_arrival(source).wait_recv()
        weight_share(source, my_half).start()
        return carry

    lax.fori_loop(1, ring, share, 0)

    def await_piece(s, carry):
        view = arrived.at[pl.ds(pl.multiple_of(s * size, size), size), :]

        @pl.when(s != c)
        def _():
            pltpu.make_async_remote_copy(
                src_ref=view,
                dst_ref=view,
                send_sem=ts_sem.at[s],
                recv_sem=tr_sem.at[s],
                device_id=(s, t),
                device_id_type=MESH,
            ).wait_recv()

        return carry

    def head_copy(g, which, send, peer):
        begin, count = bounds[g]
        view = ag.at[which, pl.ds(begin * piece, count * piece), :]
        return pltpu.make_async_remote_copy(
            src_ref=view,
            dst_ref=view,
            send_sem=xs_sem.at[g, send],
            recv_sem=xr_sem.at[g, which],
            device_id=(c, peer * 2 + y),
            device_id_type=MESH,
        )

    def term_copy(g):
        begin, count = bounds[g]
        some = pl.ds(begin * piece, count * piece)
        return pltpu.make_async_remote_copy(
            src_ref=term_out.at[some, :],
            dst_ref=term_in.at[some, :],
            send_sem=ys_sem.at[g],
            recv_sem=yr_sem.at[g],
            device_id=(c, across),
            device_id_type=MESH,
        )

    def gather_heads(g):
        begin, count = bounds[g]
        lax.fori_loop(begin, begin + count, await_piece, 0)
        split = arrived[begin * size : (begin + count) * size, :].astype(F32)
        split = split.reshape(count, 2, piece, mid)
        some = slice(begin * piece, (begin + count) * piece)
        ag[x, some, :mid] = split[:, 0].reshape(count * piece, mid).astype(BF)
        ag[x, some, mid:] = split[:, 1].reshape(count * piece, mid).astype(BF)
        for j in range(1, ring):
            dest = lax.rem(x + j, ring)
            head_copy(g, x, dest, dest).start()

    def project(g):
        begin, count = bounds[g]
        some = slice(begin * piece, (begin + count) * piece)
        for j in range(1, ring):
            source = lax.rem(x + j, ring)
            head_copy(g, source, source, source).wait_recv()

        def term(half_y):
            where = pl.ds(pl.multiple_of(half_y * cols, cols), cols)
            total = dot(ag[0, some, :], wfull[0, :, where])
            for source in range(1, ring):
                total = total + dot(ag[source, some, :], wfull[source, :, where])
            return total

        term_out[some, :] = term(1 - y).astype(BF)
        term_copy(g).start()
        acc[some, :] = term(y)

    def finish(g):
        begin, count = bounds[g]
        some = slice(begin * piece, (begin + count) * piece)
        term_copy(g).wait_recv()
        out_ref[some, :] = (acc[some, :] + term_in[some, :].astype(F32)).astype(BF)

    bounds = ((0, n // 2), (n // 2, n // 4), (n * 3 // 4, n // 4))
    gather_heads(0)
    weight_load.wait()

    def await_weights(j, carry):
        weight_share(lax.rem(x + j, ring), its_half).wait_recv()
        return carry

    lax.fori_loop(1, ring, await_weights, 0)
    gather_heads(1)
    project(0)
    gather_heads(2)
    project(1)
    project(2)
    for g in range(len(bounds)):
        finish(g)

    for g in range(len(bounds)):
        term_copy(g).wait_send()
        for j in range(1, ring):
            dest = lax.rem(x + j, ring)
            head_copy(g, x, dest, dest).wait_send()

    def drain_ctx(j, carry):
        deliver(lax.rem(c + j, n), c).wait_send()
        return carry

    lax.fori_loop(1, n, drain_ctx, 0)

    def drain_queries(k, carry):
        dispatch(k, c).wait_send()
        return carry

    lax.fori_loop(0, c, drain_queries, 0)

    def drain_back(s, carry):
        give_back(s, c).wait_send()
        return carry

    lax.fori_loop(c + 1, n, drain_back, 0)

    def drain_weights(j, carry):
        peer = lax.rem(x + j, ring)
        weight_copy(peer).wait_send()
        weight_share(peer, my_half).wait_send()
        return carry

    lax.fori_loop(1, ring, drain_weights, 0)


def local(queries, key_cache, values, out_weight, selected, shard_order):
    n, nt = lax.axis_size("ctx"), lax.axis_size("tp")
    rows, width = queries.shape
    keys = key_cache.shape[0]
    depth, model = out_weight.shape
    cols = model // nt
    pair_rows = CAP * TILE
    heads = width // DH
    dma = pltpu.SemaphoreType.DMA
    vmem = pl.BlockSpec(memory_space=pltpu.VMEM)
    hbm = pl.BlockSpec(memory_space=pl.ANY)
    return pl.pallas_call(
        functools.partial(kernel, n, nt),
        out_shape=jax.ShapeDtypeStruct((rows, cols), BF),
        in_specs=[vmem, vmem, vmem, hbm, hbm, hbm],
        out_specs=vmem,
        scratch_shapes=[
            pltpu.VMEM((keys, DH), BF),
            pltpu.VMEM((2 * DH, keys), BF),
            pltpu.VMEM((keys, 2 * DH), BF),
            pltpu.VMEM((n * pair_rows, width), BF),
            pltpu.VMEM((n, pair_rows, width), BF),
            pltpu.VMEM((n, heads * pair_rows + TILE, DH), BF),
            pltpu.VMEM((n, heads * pair_rows + TILE, DH), BF),
            pltpu.VMEM((TOPK, rows, n * pair_rows), BF),
            pltpu.VMEM((2 * rows, rows), BF),
            pltpu.VMEM((rows, width), F32),
            pltpu.VMEM((rows, width), F32),
            pltpu.VMEM((nt // 2, depth, 2 * cols), BF),
            pltpu.VMEM((2 * rows, width // 2), BF),
            pltpu.VMEM((2 * rows, width // 2), BF),
            pltpu.VMEM((nt // 2, rows, width), BF),
            pltpu.VMEM((rows, cols), BF),
            pltpu.VMEM((rows, cols), BF),
            pltpu.VMEM((rows, cols), F32),
            dma((3,)), dma((n,)), dma((n,)), dma((n,)), dma((n,)),
            dma((nt // 2,)), dma((nt // 2,)), dma((nt // 2,)), dma((nt // 2,)),
            dma((n,)), dma((n,)), dma((3,)), dma((3,)), dma((3, nt // 2)), dma((3, nt // 2)),
        ],
        compiler_params=pltpu.CompilerParams(
            collective_id=0, has_side_effects=True, vmem_limit_bytes=58 * 2**20
        ),
        name="sublayer",
    )(queries, selected.T, shard_order.reshape(1, n), key_cache, values, out_weight)


def solution(mesh):
    placed = (P("ctx", "tp"), P("ctx", "tp"), P("ctx", "tp"), P("tp", None), P("ctx", None), P())
    return jax.shard_map(
        local, mesh=mesh, in_specs=placed, out_specs=P("ctx", "tp"), check_vma=False
    )
```

time: 132 us -> 89.7 us (0.68)
  Pallas kernels: 128 us -> 86.4 us
  local copies, waits for them, and re-layouts: 3.22 us -> 1.87 us
    pallas_call x1, Pallas kernels: 128 us -> 86.4 us  [local(): pl.pallas_call(functools.partial(kernel, n, nt), out_shape=jax.ShapeDtype...]
    unnamed x2 -> x1, local copies, waits for them, and re-layouts: 3.22 us -> 1.87 us
where the time goes in v2:
time: 89.7 us; the launch traced here: 88.3 us
  Pallas kernels  86.4 us (96%)
  local copies, waits for them, and re-layouts  1.87 us (2%)
    pallas_call x1, Pallas kernels, local(): pl.pallas_call(functools.partial(kernel, n, nt), out_shape=jax.ShapeDtype...  86.4 us
    unnamed x1, local copies, waits for them, and re-layouts  1.87 us

profile of v2, /device:TPU:8, one launch (start us, length us, event | category | flops | bytes accessed | tf_op | source)
XLA Modules:
  0.0 88.3 jit_solution(1064457596166463207)
XLA Ops:
  0.0 86.4 %sublayer.1 = bf16[256,1024]{1,0:T(8,128)(2,1)} custom-call(bf16[256,512]{1,0:T(8,128)(2,1)} %q_ref.1, s32[3,16]{1,0:T(4,128)} %bitcast.2, s32[1,32]{1,0:T(1,128)} %bitcast.3, bf16[4096,128]{1,0:T(8,128)(2,1)} %k_ref.1, bf16[4096,128]{1,0:T(8,128)(2,1)} %v_ref.1, bf16[512,8192]{1,0:T(8,128)(2,1)} %w_ref.1), custom_call_target="tpu_custom_call" | custom-call | tf_op jit(solution)/shard_map/sublayer/pallas_call | solution.py:509
  86.4 1.9 %copy.8 = bf16[256,1024]{1,0:T(8,128)(2,1)} copy(bf16[256,1024]{1,0:T(8,128)(2,1)} %sublayer.1) | data formatting | bytes 1048576

commit v3 on v2

--- a/solution.py
+++ b/solution.py
@@ -87,7 +87,8 @@
         )
         return carry
 
-    lax.fori_loop(1, n, greet_ctx, 0)
+    for j in range(1, n):
+        greet_ctx(j, 0)
 
     ring = nt // 2
     x, y = t // 2, lax.rem(t, 2)
@@ -152,7 +153,7 @@
         )
 
     def send_queries(j, carry):
-        dispatch(j, c).start()
+        dispatch(c - 1 - j, c).start()
         return carry
 
     lax.fori_loop(0, c, send_queries, 0)
@@ -218,7 +219,7 @@
         ).astype(BF)
         to_slot = (iota((slots, slot_rows), 1) // TILE == iota((slots, slot_rows), 0)).astype(BF)
         same = iota((rows, slot_rows), 0) % TILE == iota((rows, slot_rows), 1) % TILE
-        pick[r] = jnp.where(same, dot(of_row, to_slot), 0.0).astype(BF)
+        pick[r * rows : (r + 1) * rows, :] = jnp.where(same, dot(of_row, to_slot), 0.0).astype(BF)
     wanted = (iota((n, n), 0) == order_ref[...]).astype(BF)
     row2 = iota((2 * rows, n), 0)
     of_shard = (row2 // (2 * piece) == iota((2 * rows, n), 1)).astype(BF)
@@ -309,23 +310,17 @@
     stats = jnp.concatenate(
         [jnp.where(stat_lane == i, stats.astype(F32), 0.0).astype(BF) for i in range(CAP)], axis=1
     ).reshape(slot_rows, DH)
+    wide = [
+        back[:, h * pair_rows : (h + 1) * pair_rows, :].reshape(slot_rows, DH) for h in range(heads)
+    ]
+    taken = dot(pick[...], jnp.concatenate(wide, axis=1))
+    taken_log = dot(dot(pick[...], stats).astype(BF), to_heads)
     logs, mixes = [own_log[...]], [own_mix[...]]
     for r in range(TOPK):
+        some = slice(r * rows, (r + 1) * rows)
         live = dot(row_of, jnp.broadcast_to((chosen[r] >= 0).astype(F32), (tiles, heads * DH)).astype(BF))
-        log_mass = dot(dot(pick[r], stats).astype(BF), to_heads)
-        logs.append(jnp.where(live > 0.5, log_mass, -1e30))
-        mixes.append(
-            jnp.concatenate(
-                [
-                    dot(
-                        pick[r],
-                        back[:, h * pair_rows : (h + 1) * pair_rows, :].reshape(slot_rows, DH),
-                    )
-                    for h in range(heads)
-                ],
-                axis=1,
-            )
-        )
+        logs.append(jnp.where(live > 0.5, taken_log[some], -1e30))
+        mixes.append(taken[some])
     top = jnp.maximum(jnp.maximum(logs[0], logs[1]), jnp.maximum(logs[2], logs[3]))
     numerator, denominator = 0.0, 0.0
     for log_mass, mix in zip(logs, mixes):
@@ -355,7 +350,8 @@
         deliver(lax.rem(c + j, n), c).start()
         return carry
 
-    lax.fori_loop(1, n, send_piece, 0)
+    for j in range(1, n):
+        send_piece(j, 0)
     here = pl.ds(pl.multiple_of(c * size, size), size)
     arrived[here, :] = pieces[here, :]
 
@@ -446,6 +442,17 @@
         out_ref[some, :] = (acc[some, :] + term_in[some, :].astype(F32)).astype(BF)
 
     bounds = ((0, n // 2), (n // 2, n // 4), (n * 3 // 4, n // 4))
+    def drain_queries(k, carry):
+        dispatch(k, c).wait_send()
+        return carry
+
+    lax.fori_loop(0, c, drain_queries, 0)
+
+    def drain_back(s, carry):
+        give_back(s, c).wait_send()
+        return carry
+
+    lax.fori_loop(c + 1, n, drain_back, 0)
     gather_heads(0)
     weight_load.wait()
 
@@ -457,6 +464,11 @@
     gather_heads(1)
     project(0)
     gather_heads(2)
+    def drain_ctx(j, carry):
+        deliver(lax.rem(c + j, n), c).wait_send()
+        return carry
+
+    lax.fori_loop(1, n, drain_ctx, 0)
     project(1)
     project(2)
     for g in range(len(bounds)):
@@ -467,24 +479,6 @@
         for j in range(1, ring):
             dest = lax.rem(x + j, ring)
             head_copy(g, x, dest, dest).wait_send()
-
-    def drain_ctx(j, carry):
-        deliver(lax.rem(c + j, n), c).wait_send()
-        return carry
-
-    lax.fori_loop(1, n, drain_ctx, 0)
-
-    def drain_queries(k, carry):
-        dispatch(k, c).wait_send()
-        return carry
-
-    lax.fori_loop(0, c, drain_queries, 0)
-
-    def drain_back(s, carry):
-        give_back(s, c).wait_send()
-        return carry
-
-    lax.fori_loop(c + 1, n, drain_back, 0)
 
     def drain_weights(j, carry):
         peer = lax.rem(x + j, ring)
@@ -519,7 +513,7 @@
             pltpu.VMEM((n, pair_rows, width), BF),
             pltpu.VMEM((n, heads * pair_rows + TILE, DH), BF),
             pltpu.VMEM((n, heads * pair_rows + TILE, DH), BF),
-            pltpu.VMEM((TOPK, rows, n * pair_rows), BF),
+            pltpu.VMEM((TOPK * rows, n * pair_rows), BF),
             pltpu.VMEM((2 * rows, rows), BF),
             pltpu.VMEM((rows, width), F32),
             pltpu.VMEM((rows, width), F32),

time: 89.7 us -> 85.4 us (0.952)
  Pallas kernels: 86.4 us -> 82.4 us
    pallas_call x1, Pallas kernels: 86.4 us -> 82.4 us  [local(): pl.pallas_call(functools.partial(kernel, n, nt), out_shape=jax.ShapeDtype...]
where the time goes in v3:
time: 85.4 us; the launch traced here: 84.2 us
  Pallas kernels  82.4 us (96%)
  local copies, waits for them, and re-layouts  1.87 us (2%)
    pallas_call x1, Pallas kernels, local(): pl.pallas_call(functools.partial(kernel, n, nt), out_shape=jax.ShapeDtype...  82.4 us
    unnamed x1, local copies, waits for them, and re-layouts  1.87 us

profile of v3, /device:TPU:8, one launch (start us, length us, event | category | flops | bytes accessed | tf_op | source)
XLA Modules:
  0.0 84.2 jit_solution(16985911030103668667)
XLA Ops:
  0.0 82.4 %sublayer.1 = bf16[256,1024]{1,0:T(8,128)(2,1)} custom-call(bf16[256,512]{1,0:T(8,128)(2,1)} %q_ref.1, s32[3,16]{1,0:T(4,128)} %bitcast.2, s32[1,32]{1,0:T(1,128)} %bitcast.3, bf16[4096,128]{1,0:T(8,128)(2,1)} %k_ref.1, bf16[4096,128]{1,0:T(8,128)(2,1)} %v_ref.1, bf16[512,8192]{1,0:T(8,128)(2,1)} %w_ref.1), custom_call_target="tpu_custom_call" | custom-call | tf_op jit(solution)/shard_map/sublayer/pallas_call | solution.py:503
  82.4 1.9 %copy.8 = bf16[256,1024]{1,0:T(8,128)(2,1)} copy(bf16[256,1024]{1,0:T(8,128)(2,1)} %sublayer.1) | data formatting | bytes 1048576

commit v4 on v3

--- a/solution.py
+++ b/solution.py
@@ -417,6 +417,13 @@
             dest = lax.rem(x + j, ring)
             head_copy(g, x, dest, dest).start()
 
+    def term(some, half_y):
+        where = pl.ds(pl.multiple_of(half_y * cols, cols), cols)
+        total = dot(ag[0, some, :], wfull[0, :, where])
+        for source in range(1, ring):
+            total = total + dot(ag[source, some, :], wfull[source, :, where])
+        return total
+
     def project(g):
         begin, count = bounds[g]
         some = slice(begin * piece, (begin + count) * piece)
@@ -424,16 +431,8 @@
             source = lax.rem(x + j, ring)
             head_copy(g, source, source, source).wait_recv()
 
-        def term(half_y):
-            where = pl.ds(pl.multiple_of(half_y * cols, cols), cols)
-            total = dot(ag[0, some, :], wfull[0, :, where])
-            for source in range(1, ring):
-                total = total + dot(ag[source, some, :], wfull[source, :, where])
-            return total
-
-        term_out[some, :] = term(1 - y).astype(BF)
+        term_out[some, :] = term(some, 1 - y).astype(BF)
         term_copy(g).start()
-        acc[some, :] = term(y)
 
     def finish(g):
         begin, count = bounds[g]
@@ -464,13 +463,14 @@
     gather_heads(1)
     project(0)
     gather_heads(2)
+    project(1)
+    project(2)
     def drain_ctx(j, carry):
         deliver(lax.rem(c + j, n), c).wait_send()
         return carry
 
     lax.fori_loop(1, n, drain_ctx, 0)
-    project(1)
-    project(2)
+    acc[...] = term(slice(0, rows), y)
     for g in range(len(bounds)):
         finish(g)
 

time: 85.4 us -> 85.4 us (level)
  no operation moved by 1% of the time
where the time goes in v4:
time: 85.4 us; the launch traced here: 84.2 us
  Pallas kernels  82.4 us (96%)
  local copies, waits for them, and re-layouts  1.87 us (2%)
    pallas_call x1, Pallas kernels, local(): pl.pallas_call(functools.partial(kernel, n, nt), out_shape=jax.ShapeDtype...  82.4 us
    unnamed x1, local copies, waits for them, and re-layouts  1.87 us

profile of v4, /device:TPU:8, one launch (start us, length us, event | category | flops | bytes accessed | tf_op | source)
XLA Modules:
  0.0 84.2 jit_solution(16525945603582508874)
XLA Ops:
  0.0 82.4 %sublayer.1 = bf16[256,1024]{1,0:T(8,128)(2,1)} custom-call(bf16[256,512]{1,0:T(8,128)(2,1)} %q_ref.1, s32[3,16]{1,0:T(4,128)} %bitcast.2, s32[1,32]{1,0:T(1,128)} %bitcast.3, bf16[4096,128]{1,0:T(8,128)(2,1)} %k_ref.1, bf16[4096,128]{1,0:T(8,128)(2,1)} %v_ref.1, bf16[512,8192]{1,0:T(8,128)(2,1)} %w_ref.1), custom_call_target="tpu_custom_call" | custom-call | tf_op jit(solution)/shard_map/sublayer/pallas_call | solution.py:503
  82.4 1.9 %copy.8 = bf16[256,1024]{1,0:T(8,128)(2,1)} copy(bf16[256,1024]{1,0:T(8,128)(2,1)} %sublayer.1) | data formatting | bytes 1048576

commit v5 on v3

--- a/solution.py
+++ b/solution.py
@@ -441,7 +441,8 @@
         term_copy(g).wait_recv()
         out_ref[some, :] = (acc[some, :] + term_in[some, :].astype(F32)).astype(BF)
 
-    bounds = ((0, n // 2), (n // 2, n // 4), (n * 3 // 4, n // 4))
+    cuts = (0, n * 9 // 16, n * 13 // 16, n)
+    bounds = tuple((a, b - a) for a, b in zip(cuts, cuts[1:]))
     def drain_queries(k, carry):
         dispatch(k, c).wait_send()
         return carry

time: 85.4 us -> 86.6 us (1.014)
  no operation moved by 1% of the time
where the time goes in v5:
time: 86.6 us; the launch traced here: 85 us
  Pallas kernels  83.1 us (96%)
  local copies, waits for them, and re-layouts  1.87 us (2%)
    pallas_call x1, Pallas kernels, local(): pl.pallas_call(functools.partial(kernel, n, nt), out_shape=jax.ShapeDtype...  83.1 us
    unnamed x1, local copies, waits for them, and re-layouts  1.87 us

profile of v5, /device:TPU:8, one launch (start us, length us, event | category | flops | bytes accessed | tf_op | source)
XLA Modules:
  0.0 85.0 jit_solution(17852213428769993552)
XLA Ops:
  0.0 83.1 %sublayer.1 = bf16[256,1024]{1,0:T(8,128)(2,1)} custom-call(bf16[256,512]{1,0:T(8,128)(2,1)} %q_ref.1, s32[3,16]{1,0:T(4,128)} %bitcast.2, s32[1,32]{1,0:T(1,128)} %bitcast.3, bf16[4096,128]{1,0:T(8,128)(2,1)} %k_ref.1, bf16[4096,128]{1,0:T(8,128)(2,1)} %v_ref.1, bf16[512,8192]{1,0:T(8,128)(2,1)} %w_ref.1), custom_call_target="tpu_custom_call" | custom-call | tf_op jit(solution)/shard_map/sublayer/pallas_call | solution.py:504
  83.2 1.9 %copy.8 = bf16[256,1024]{1,0:T(8,128)(2,1)} copy(bf16[256,1024]{1,0:T(8,128)(2,1)} %sublayer.1) | data formatting | bytes 1048576
